TPU v7x, 128 devices: a whole 4x4x4 slice. The times are simulated.
128 devices in a mesh: ctx: 64 (over z, y_hi, x, core), tp: 2 (over y_lo).
Axes of the slice: x: 4, y: 4 (y_hi: 2, y_lo: 2; y = y_hi * 2 + y_lo), z: 4, core: 2. Of those that a mesh axis runs over, the one named last changes fastest.
Arguments:
- query_gate: bfloat16 [32768, 4096], P('ctx', 'tp'), may hold values from -6 to 6
- key_gate: bfloat16 [32768, 4096], P('ctx', 'tp'), may hold values from -6 to 6
- value_input: bfloat16 [32768, 4096], P('ctx', 'tp'), may hold values from -6 to 6
- decay_rates: float32 [16, 4096], P(None, 'tp'), may hold values from 3.0517577e-07 to 0.05
- residues: float32 [16, 4096], P(None, 'tp'), may hold values from -1.5 to 1.5
- skip_gain: float32 [4096], P('tp'), may hold values from -4 to 4
- out_weight: bfloat16 [4096, 4096], P('tp'), may hold values from -0.09375 to 0.09375
Outputs:
- mixed: bfloat16 [32768, 4096], P('ctx', 'tp')
All inputs are finite; a program needn't handle non-finite values.
Results may differ from a plain program's by a relative error of at most 0.005.
Values sent between devices are 32-bit elements; how exact they have to be, the bound alone decides.
A program may use at most 320 MiB of HBM per device.

v0:
```python
import jax
import jax.numpy as jnp
from jax import lax
from jax.experimental import pallas as pl
from jax.experimental.pallas import tpu as pltpu
from jax.sharding import PartitionSpec as P

MESH = pl.DeviceIdType.MESH
F32 = jnp.float32
BF16 = jnp.bfloat16

ROWS = 512
CHAN = 2048
COLS = 2048
MODES = 16
LANES = 128
NB = 8
NJ = ROWS // NB
NCG = CHAN // LANES
SHARES = 8
CPS = NCG // SHARES
JPC = 8
NCHUNK = NJ // JPC
CROWS = JPC * NB
TILE = 512
NT = COLS // TILE
LPT = TILE // LANES


def one_minus_exp_neg(y):
    series = jnp.ones_like(y)
    for k in range(10, 1, -1):
        series = 1.0 - y * series * (1.0 / k)
    return jnp.where(y < 0.5, y * series, 1.0 - jnp.exp(-y))


def spread(x):
    return jnp.broadcast_to(x[:, None, :], (MODES, NB, LANES))


def kernel(
    q_hbm, k_hbm, v_hbm, lam_hbm, res_hbm, skip_hbm, w_hbm, out_hbm,
    qb, kb, vb, lam, res, skip, wv, prod, gate, gated, send_p, recv_p, own_p, out_v,
    a_s, w_s, pw_s, state, ends, recv1, recv2, recv3, send2, send3,
    in_sem, w_sem, out_sem, s1, r1, s2, r2, s3, r3, sp, rp,
):
    c = lax.axis_index("ctx")
    t = lax.axis_index("tp")
    member = lax.rem(c, 8)
    yh = lax.rem(c // 8, 2)
    z = c // 16
    group = z * 2 + yh
    base = c - member

    def member_dev(m):
        return (base + m, t)

    def group_dev(g):
        return (g * 8 + member, t)

    partner = (c, 1 - t)

    def lanes(cg):
        return pl.ds(pl.multiple_of(cg * LANES, LANES), LANES)

    def share_cols(s):
        return pl.ds(pl.multiple_of(s * (CPS * LANES), CPS * LANES), CPS * LANES)

    small = [
        pltpu.make_async_copy(lam_hbm, lam, in_sem.at[3, 0]),
        pltpu.make_async_copy(res_hbm, res, in_sem.at[3, 1]),
        pltpu.make_async_copy(skip_hbm, skip, in_sem.at[3, 2]),
    ]
    for cp in small:
        cp.start()

    def load(which, hbm, dst, s):
        return pltpu.make_async_copy(hbm.at[:, share_cols(s)], dst.at[:, share_cols(s)], in_sem.at[which, s])

    for s in range(SHARES):
        load(0, k_hbm, kb, s).start()
        load(1, v_hbm, vb, s).start()

    barrier = pltpu.get_barrier_semaphore()
    for i in range(1, 8):
        pl.semaphore_signal(barrier, inc=1, device_id=member_dev(lax.rem(member + i, 8)), device_id_type=MESH)
        pl.semaphore_signal(barrier, inc=1, device_id=group_dev(lax.rem(group + i, 8)), device_id_type=MESH)
    pl.semaphore_signal(barrier, inc=1, device_id=partner, device_id_type=MESH)

    for cp in small:
        cp.wait()
    pl.semaphore_wait(barrier, 15)

    sub = lax.broadcasted_iota(jnp.int32, (MODES, NB, LANES), 1)

    def first_pass(s, _):
        load(0, k_hbm, kb, s).wait()
        load(1, v_hbm, vb, s).wait()

        def group_pass(u, _):
            cg = s * CPS + u
            cols = lanes(cg)
            rate = lam[:, cols]
            a = spread(jnp.exp(-rate))
            a_s[cg] = a
            for b in range(NB):
                rows = pl.ds(b * NJ, NJ)
                prod[cg, pl.ds(b, NJ, stride=NB), :] = kb[rows, cols].astype(F32) * vb[rows, cols].astype(F32)

            def step(j, acc):
                p = prod[cg, pl.ds(pl.multiple_of(j * NB, NB), NB), :]
                return acc * a + p[None]

            acc = lax.fori_loop(0, NJ, step, jnp.zeros((MODES, NB, LANES), F32), unroll=8)
            d1 = spread(jnp.exp(-float(NJ) * rate))
            d2 = d1 * d1
            acc = acc + jnp.where(sub >= 1, d1 * pltpu.roll(acc, 1, 1), 0.0)
            acc = acc + jnp.where(sub >= 2, d2 * pltpu.roll(acc, 2, 1), 0.0)
            acc = acc + jnp.where(sub >= 4, d2 * d2 * pltpu.roll(acc, 4, 1), 0.0)
            state[cg] = jnp.where(sub >= 1, pltpu.roll(acc, 1, 1), 0.0)
            ends[s, u] = acc[:, NB - 1, :]
            return 0

        lax.fori_loop(0, CPS, group_pass, 0)

        @pl.when(s != member)
        def _():
            pltpu.make_async_remote_copy(
                src_ref=ends.at[s], dst_ref=recv1.at[member], send_sem=s1.at[s], recv_sem=r1.at[member],
                device_id=member_dev(s), device_id_type=MESH,
            ).start()

        @pl.when(s == member)
        def _():
            recv1[member] = ends[s]

        return 0

    lax.fori_loop(0, SHARES, first_pass, 0)

    def load_w(half, n):
        start = (1 - t if half == 0 else t) * COLS + n * TILE
        cols = pl.ds(pl.multiple_of(start, TILE), TILE)
        return pltpu.make_async_copy(w_hbm.at[:, cols], wv.at[half, n], w_sem.at[half, n])

    for s in range(SHARES):
        load(2, q_hbm, qb, s).start()
    for half in range(2):
        for n in range(NT):
            load_w(half, n).start()

    def share_decay(span):
        return jnp.exp(-float(span) * lam[:, share_cols(member)])

    def halves(x):
        return jnp.stack([x[:, u * LANES:(u + 1) * LANES] for u in range(CPS)])

    d_dev = halves(share_decay(ROWS))
    d_grp = halves(share_decay(ROWS * 8))

    def wait_recv(buf, sem, i, ssem):
        pltpu.make_async_remote_copy(
            src_ref=buf.at[i], dst_ref=buf.at[i], send_sem=ssem.at[i], recv_sem=sem.at[i],
            device_id=partner, device_id_type=MESH,
        ).wait_recv()

    for i in range(1, 8):
        m = lax.rem(member + i, 8)
        wait_recv(recv1, r1, m, s1)
    total = recv1[0]
    for m in range(1, 8):
        total = total * d_dev + recv1[m]
    send2[...] = total
    recv2[group] = total

    def copy2(g):
        return pltpu.make_async_remote_copy(
            src_ref=send2, dst_ref=recv2.at[group], send_sem=s2.at[g], recv_sem=r2.at[group],
            device_id=group_dev(g), device_id_type=MESH,
        )

    for i in (4, 5, 3, 6, 2, 7, 1):
        copy2(lax.rem(group + i, 8)).start()

    def prepare(cg, _):
        cols = lanes(cg)
        rate = lam[:, cols]
        w_s[cg] = spread(res[:, cols] * jnp.sqrt(one_minus_exp_neg(2.0 * rate)))
        pw_s[cg] = jnp.exp(spread(rate) * (sub.astype(F32) * -float(NJ)))
        for b in range(NB):
            gate[cg, pl.ds(b, NJ, stride=NB), :] = qb[pl.ds(b * NJ, NJ), cols].astype(F32)
        return 0

    for s in range(SHARES):
        load(2, q_hbm, qb, s).wait()
    lax.fori_loop(0, NCG, prepare, 0)

    for i in (1, 7, 2, 6, 3, 5, 4):
        wait_recv(recv2, r2, lax.rem(group + i, 8), s2)
    incoming = jnp.zeros((CPS, MODES, LANES), F32)
    for g in range(8):
        incoming = jnp.where(g < group, incoming * d_grp + recv2[g], incoming)
    for m in range(8):
        send3[m] = incoming
        if m < 7:
            incoming = incoming * d_dev + recv1[m]
    recv3[member] = send3[member]

    def copy3(m):
        return pltpu.make_async_remote_copy(
            src_ref=send3.at[m], dst_ref=recv3.at[member], send_sem=s3.at[m], recv_sem=r3.at[member],
            device_id=member_dev(m), device_id_type=MESH,
        )

    for i in (4, 5, 3, 6, 2, 7, 1):
        copy3(lax.rem(member + i, 8)).start()

    def second_pass(chunk, cg):
        cols = lanes(cg)
        a = a_s[cg]
        w = w_s[cg]
        gain = skip[:, cols]
        x = state[cg]
        for pair in range(JPC // 2):
            tiles = []
            for j in (2 * pair, 2 * pair + 1):
                rows = pl.ds(pl.multiple_of((chunk * JPC + j) * NB, NB), NB)
                p = prod[cg, rows, :]
                x = x * a + p[None]
                filtered = jnp.sum(x * w, axis=0) + gain * p
                tiles.append(gate[cg, rows, :] * filtered)
            rows = pl.ds(pl.multiple_of(chunk * CROWS + pair * 16, 16), 16)
            gated[rows, cols] = jnp.concatenate(tiles, axis=0).astype(BF16)
        state[cg] = x

    def chunk_rows(chunk):
        return pl.ds(pl.multiple_of(chunk * CROWS, CROWS), CROWS)

    def tile_lanes(n):
        return pl.ds(n * LPT, LPT)

    def piece(chunk, n):
        return pltpu.make_async_remote_copy(
            src_ref=send_p.at[tile_lanes(n), chunk_rows(chunk)], dst_ref=recv_p.at[tile_lanes(n), chunk_rows(chunk)],
            send_sem=sp.at[chunk, n], recv_sem=rp.at[chunk, n], device_id=partner, device_id_type=MESH,
        )

    def project(chunk):
        rows = chunk_rows(chunk)

        def other(n, _):
            sums = jnp.dot(gated[rows, :], wv[0, n], preferred_element_type=F32)
            for u in range(LPT):
                send_p[n * LPT + u, rows, :] = sums[:, u * LANES:(u + 1) * LANES]
            piece(chunk, n).start()
            return 0

        lax.fori_loop(0, NT, other, 0)

    def project_own(chunk):
        rows = chunk_rows(chunk)

        def own(n, _):
            sums = jnp.dot(gated[rows, :], wv[1, n], preferred_element_type=F32)
            for u in range(LPT):
                own_p[n * LPT + u, rows, :] = sums[:, u * LANES:(u + 1) * LANES]
            return 0

        lax.fori_loop(0, NT, own, 0)

    for i in range(8):
        s = lax.rem(member + i, 8)
        if i > 0:
            wait_recv(recv3, r3, s, s3)

        def start(u, _, s=s):
            cg = s * CPS + u
            state[cg] = state[cg] + pw_s[cg] * spread(recv3[s, u])
            second_pass(0, cg)
            return 0

        lax.fori_loop(0, CPS, start, 0)

    for n in range(NT):
        load_w(0, n).wait()
    project(0)
    for n in range(NT):
        load_w(1, n).wait()
    project_own(0)

    def chunk_step(chunk, _):
        def one(cg, _):
            second_pass(chunk, cg)
            return 0

        lax.fori_loop(0, NCG, one, 0)
        project(chunk)
        project_own(chunk)
        return 0

    lax.fori_loop(1, NCHUNK, chunk_step, 0)

    def store(h, n):
        cols = pl.ds(pl.multiple_of(n * TILE, TILE), TILE)
        rows = pl.ds(pl.multiple_of(h * 16, 16), 16)
        return pltpu.make_async_copy(out_v.at[:, rows, cols], out_hbm.at[:, rows, cols], out_sem.at[h, n])

    def finish(i, _):
        h, n = i // NT, lax.rem(i, NT)
        cols = pl.ds(pl.multiple_of(n * TILE, TILE), TILE)
        piece(2 * h, n).wait_recv()
        piece(2 * h + 1, n).wait_recv()

        for u in range(LPT):
            k = n * LPT + u
            for b in range(NB):
                rows = pl.ds(h * (2 * CROWS) + b, 16, stride=NB)
                out_v[b, pl.ds(pl.multiple_of(h * 16, 16), 16), lanes(k)] = (own_p[k, rows, :] + recv_p[k, rows, :]).astype(BF16)
        store(h, n).start()
        return 0

    lax.fori_loop(0, (NCHUNK // 2) * NT, finish, 0)

    for i in range(1, 8):
        m = lax.rem(member + i, 8)
        g = lax.rem(group + i, 8)
        pltpu.make_async_remote_copy(
            src_ref=ends.at[m], dst_ref=recv1.at[member], send_sem=s1.at[m], recv_sem=r1.at[member],
            device_id=member_dev(m), device_id_type=MESH,
        ).wait_send()
        copy2(g).wait_send()
        copy3(m).wait_send()

    def drain(i, _):
        piece(i // NT, lax.rem(i, NT)).wait_send()
        return 0

    lax.fori_loop(0, NCHUNK * NT, drain, 0)

    def stored(i, _):
        store(i // NT, lax.rem(i, NT)).wait()
        return 0

    lax.fori_loop(0, (NCHUNK // 2) * NT, stored, 0)


def per_device(query_gate, key_gate, value_input, decay_rates, residues, skip_gain, out_weight):
    dma = pltpu.SemaphoreType.DMA
    out = pl.pallas_call(
        kernel,
        out_shape=jax.ShapeDtypeStruct((NB, NJ, COLS), BF16),
        in_specs=[pl.BlockSpec(memory_space=pl.ANY)] * 7,
        out_specs=pl.BlockSpec(memory_space=pl.ANY),
        scratch_shapes=[
            pltpu.VMEM((ROWS, CHAN), BF16),
            pltpu.VMEM((ROWS, CHAN), BF16),
            pltpu.VMEM((ROWS, CHAN), BF16),
            pltpu.VMEM((MODES, CHAN), F32),
            pltpu.VMEM((MODES, CHAN), F32),
            pltpu.VMEM((1, CHAN), F32),
            pltpu.VMEM((2, NT, CHAN, TILE), BF16),
            pltpu.VMEM((NCG, ROWS, LANES), F32),
            pltpu.VMEM((NCG, ROWS, LANES), F32),
            pltpu.VMEM((ROWS, CHAN), BF16),
            pltpu.VMEM((COLS // LANES, ROWS, LANES), F32),
            pltpu.VMEM((COLS // LANES, ROWS, LANES), F32),
            pltpu.VMEM((COLS // LANES, ROWS, LANES), F32),
            pltpu.VMEM((NB, NJ, COLS), BF16),
            pltpu.VMEM((NCG, MODES, NB, LANES), F32),
            pltpu.VMEM((NCG, MODES, NB, LANES), F32),
            pltpu.VMEM((NCG, MODES, NB, LANES), F32),
            pltpu.VMEM((NCG, MODES, NB, LANES), F32),
            pltpu.VMEM((SHARES, CPS, MODES, LANES), F32),
            pltpu.VMEM((8, CPS, MODES, LANES), F32),
            pltpu.VMEM((8, CPS, MODES, LANES), F32),
            pltpu.VMEM((8, CPS, MODES, LANES), F32),
            pltpu.VMEM((CPS, MODES, LANES), F32),
            pltpu.VMEM((8, CPS, MODES, LANES), F32),
            dma((4, SHARES)), dma((2, NT)), dma((NCHUNK // 2, NT)),
            dma((8,)), dma((8,)), dma((8,)), dma((8,)), dma((8,)), dma((8,)),
            dma((NCHUNK, NT)), dma((NCHUNK, NT)),
        ],
        compiler_params=pltpu.CompilerParams(
            collective_id=0, has_side_effects=True, vmem_limit_bytes=60 * 2**20
        ),
    )(
        query_gate, key_gate, value_input, decay_rates, residues, skip_gain.reshape(1, CHAN), out_weight
    )
    return out.reshape(ROWS, COLS)


def solution(mesh):
    in_specs = (
        P("ctx", "tp"),
        P("ctx", "tp"),
        P("ctx", "tp"),
        P(None, "tp"),
        P(None, "tp"),
        P("tp"),
        P("tp", None),
    )
    return jax.shard_map(per_device, mesh=mesh, in_specs=in_specs, out_specs=P("ctx", "tp"), check_vma=False)
```

profile of v0, /device:TPU:1, one launch (start us, length us, event | category | flops | bytes accessed | tf_op | source)
XLA Modules:
  0.0 125.7 jit_solution(4476294187275501335)
XLA Ops:
  0.0 122.5 %shard_map.73 = bf16[8,64,2048]{2,1,0:T(8,128)(2,1)} custom-call(bf16[512,2048]{1,0:T(8,128)(2,1)} %q_hbm.1, bf16[512,2048]{1,0:T(8,128)(2,1)} %k_hbm.1, bf16[512,2048]{1,0:T(8,128)(2,1)} %v_hbm.1, f32[16,2048]{1,0:T(8,128)} %lam_hbm.1, f32[16,2048]{1,0:T(8,128)} %res_hbm.1, f32[1,2048]{1,0:T(1,128)} %bitcast.3, bf16[2048,4096]{1,0:T(8,128)(2,1)} %w_hbm.1), custom_call_target="tpu_custom_call" | custom-call | tf_op jit(solution)/shard_map/pallas_call | solution.py:349
  122.5 3.2 %copy.9 = bf16[512,2048]{1,0:T(8,128)(2,1)} copy(bf16[512,2048]{1,0:T(8,128)(2,1)} %bitcast.2) | data formatting | bytes 4194304
where the time goes:
time: 126 us
  Pallas kernels  122 us (97%)
  local copies, waits for them, and re-layouts  3.16 us (3%)
    pallas_call x1, Pallas kernels, per_device(): pl.pallas_call(kernel, out_shape=jax.ShapeDtypeStruct((NB, NJ, COLS), BF1...  122 us
    unnamed x1, local copies, waits for them, and re-layouts  3.16 us

commit v1 on v0

--- a/solution.py
+++ b/solution.py
@@ -25,6 +25,8 @@
 TILE = 512
 NT = COLS // TILE
 LPT = TILE // LANES
+EARLY = 4
+SPLIT1, SPLIT2 = 6, 15
 
 
 def one_minus_exp_neg(y):
@@ -39,10 +41,10 @@
 
 
 def kernel(
-    q_hbm, k_hbm, v_hbm, lam_hbm, res_hbm, skip_hbm, w_hbm, out_hbm,
-    qb, kb, vb, lam, res, skip, wv, prod, gate, gated, send_p, recv_p, own_p, out_v,
+    q_hbm, k_hbm, v_hbm, lam_hbm, res_hbm, skip_hbm, w_hbm, out_v,
+    qb, kb, vb, lam, res, skip, wv, prod, gate, gated, send_p, recv_p, own_p,
     a_s, w_s, pw_s, state, ends, recv1, recv2, recv3, send2, send3,
-    in_sem, w_sem, out_sem, s1, r1, s2, r2, s3, r3, sp, rp,
+    in_sem, w_sem, s1, r1, s2, r2, s3, r3, sp, rp,
 ):
     c = lax.axis_index("ctx")
     t = lax.axis_index("tp")
@@ -89,40 +91,31 @@
 
     for cp in small:
         cp.wait()
-    pl.semaphore_wait(barrier, 15)
 
     sub = lax.broadcasted_iota(jnp.int32, (MODES, NB, LANES), 1)
 
-    def first_pass(s, _):
+    def end_state(s):
         load(0, k_hbm, kb, s).wait()
         load(1, v_hbm, vb, s).wait()
 
         def group_pass(u, _):
-            cg = s * CPS + u
-            cols = lanes(cg)
+            cols = lanes(s * CPS + u)
             rate = lam[:, cols]
-            a = spread(jnp.exp(-rate))
-            a_s[cg] = a
-            for b in range(NB):
-                rows = pl.ds(b * NJ, NJ)
-                prod[cg, pl.ds(b, NJ, stride=NB), :] = kb[rows, cols].astype(F32) * vb[rows, cols].astype(F32)
-
-            def step(j, acc):
-                p = prod[cg, pl.ds(pl.multiple_of(j * NB, NB), NB), :]
-                return acc * a + p[None]
-
-            acc = lax.fori_loop(0, NJ, step, jnp.zeros((MODES, NB, LANES), F32), unroll=8)
-            d1 = spread(jnp.exp(-float(NJ) * rate))
-            d2 = d1 * d1
-            acc = acc + jnp.where(sub >= 1, d1 * pltpu.roll(acc, 1, 1), 0.0)
-            acc = acc + jnp.where(sub >= 2, d2 * pltpu.roll(acc, 2, 1), 0.0)
-            acc = acc + jnp.where(sub >= 4, d2 * d2 * pltpu.roll(acc, 4, 1), 0.0)
-            state[cg] = jnp.where(sub >= 1, pltpu.roll(acc, 1, 1), 0.0)
-            ends[s, u] = acc[:, NB - 1, :]
+            a8 = spread(jnp.exp(-8.0 * rate))
+
+            def step(i, acc):
+                rows = pl.ds(pl.multiple_of(i * 16, 16), 16)
+                p = kb[rows, cols].astype(F32) * vb[rows, cols].astype(F32)
+                acc = acc * a8 + p[None, :8]
+                return acc * a8 + p[None, 8:]
+
+            acc = lax.fori_loop(0, ROWS // 16, step, jnp.zeros((MODES, NB, LANES), F32), unroll=8)
+            ends[s, u] = jnp.sum(acc * jnp.exp(spread(rate) * (sub - 7).astype(F32)), axis=1)
             return 0
 
         lax.fori_loop(0, CPS, group_pass, 0)
 
+    def give_share(s):
         @pl.when(s != member)
         def _():
             pltpu.make_async_remote_copy(
@@ -134,9 +127,19 @@
         def _():
             recv1[member] = ends[s]
 
-        return 0
-
-    lax.fori_loop(0, SHARES, first_pass, 0)
+    def first_half(s, _):
+        end_state(s)
+        return 0
+
+    def second_half(s, _):
+        end_state(s)
+        give_share(s)
+        return 0
+
+    lax.fori_loop(0, EARLY, first_half, 0)
+    pl.semaphore_wait(barrier, 15)
+    for s in range(EARLY):
+        give_share(s)
 
     def load_w(half, n):
         start = (1 - t if half == 0 else t) * COLS + n * TILE
@@ -148,6 +151,32 @@
     for half in range(2):
         for n in range(NT):
             load_w(half, n).start()
+
+    lax.fori_loop(EARLY, SHARES, second_half, 0)
+
+    def block_states(cg, _):
+        cols = lanes(cg)
+        rate = lam[:, cols]
+        a = spread(jnp.exp(-rate))
+        a_s[cg] = a
+        for b in range(NB):
+            rows = pl.ds(b * NJ, NJ)
+            prod[cg, pl.ds(b, NJ, stride=NB), :] = kb[rows, cols].astype(F32) * vb[rows, cols].astype(F32)
+
+        def step(j, acc):
+            p = prod[cg, pl.ds(pl.multiple_of(j * NB, NB), NB), :]
+            return acc * a + p[None]
+
+        acc = lax.fori_loop(0, NJ, step, jnp.zeros((MODES, NB, LANES), F32), unroll=16)
+        d1 = spread(jnp.exp(-float(NJ) * rate))
+        d2 = d1 * d1
+        acc = acc + jnp.where(sub >= 1, d1 * pltpu.roll(acc, 1, 1), 0.0)
+        acc = acc + jnp.where(sub >= 2, d2 * pltpu.roll(acc, 2, 1), 0.0)
+        acc = acc + jnp.where(sub >= 4, d2 * d2 * pltpu.roll(acc, 4, 1), 0.0)
+        state[cg] = jnp.where(sub >= 1, pltpu.roll(acc, 1, 1), 0.0)
+        return 0
+
+    lax.fori_loop(0, SPLIT1, block_states, 0)
 
     def share_decay(span):
         return jnp.exp(-float(span) * lam[:, share_cols(member)])
@@ -182,18 +211,7 @@
     for i in (4, 5, 3, 6, 2, 7, 1):
         copy2(lax.rem(group + i, 8)).start()
 
-    def prepare(cg, _):
-        cols = lanes(cg)
-        rate = lam[:, cols]
-        w_s[cg] = spread(res[:, cols] * jnp.sqrt(one_minus_exp_neg(2.0 * rate)))
-        pw_s[cg] = jnp.exp(spread(rate) * (sub.astype(F32) * -float(NJ)))
-        for b in range(NB):
-            gate[cg, pl.ds(b, NJ, stride=NB), :] = qb[pl.ds(b * NJ, NJ), cols].astype(F32)
-        return 0
-
-    for s in range(SHARES):
-        load(2, q_hbm, qb, s).wait()
-    lax.fori_loop(0, NCG, prepare, 0)
+    lax.fori_loop(SPLIT1, SPLIT2, block_states, 0)
 
     for i in (1, 7, 2, 6, 3, 5, 4):
         wait_recv(recv2, r2, lax.rem(group + i, 8), s2)
@@ -214,6 +232,21 @@
 
     for i in (4, 5, 3, 6, 2, 7, 1):
         copy3(lax.rem(member + i, 8)).start()
+
+    lax.fori_loop(SPLIT2, NCG, block_states, 0)
+
+    def prepare(cg, _):
+        cols = lanes(cg)
+        rate = lam[:, cols]
+        w_s[cg] = spread(res[:, cols] * jnp.sqrt(one_minus_exp_neg(2.0 * rate)))
+        pw_s[cg] = jnp.exp(spread(rate) * (sub.astype(F32) * -float(NJ)))
+        for b in range(NB):
+            gate[cg, pl.ds(b, NJ, stride=NB), :] = qb[pl.ds(b * NJ, NJ), cols].astype(F32)
+        return 0
+
+    for s in range(SHARES):
+        load(2, q_hbm, qb, s).wait()
+    lax.fori_loop(0, NCG, prepare, 0)
 
     def second_pass(chunk, cg):
         cols = lanes(cg)
@@ -300,14 +333,8 @@
 
     lax.fori_loop(1, NCHUNK, chunk_step, 0)
 
-    def store(h, n):
-        cols = pl.ds(pl.multiple_of(n * TILE, TILE), TILE)
-        rows = pl.ds(pl.multiple_of(h * 16, 16), 16)
-        return pltpu.make_async_copy(out_v.at[:, rows, cols], out_hbm.at[:, rows, cols], out_sem.at[h, n])
-
     def finish(i, _):
         h, n = i // NT, lax.rem(i, NT)
-        cols = pl.ds(pl.multiple_of(n * TILE, TILE), TILE)
         piece(2 * h, n).wait_recv()
         piece(2 * h + 1, n).wait_recv()
 
@@ -316,7 +343,6 @@
             for b in range(NB):
                 rows = pl.ds(h * (2 * CROWS) + b, 16, stride=NB)
                 out_v[b, pl.ds(pl.multiple_of(h * 16, 16), 16), lanes(k)] = (own_p[k, rows, :] + recv_p[k, rows, :]).astype(BF16)
-        store(h, n).start()
         return 0
 
     lax.fori_loop(0, (NCHUNK // 2) * NT, finish, 0)
@@ -337,20 +363,14 @@
 
     lax.fori_loop(0, NCHUNK * NT, drain, 0)
 
-    def stored(i, _):
-        store(i // NT, lax.rem(i, NT)).wait()
-        return 0
-
-    lax.fori_loop(0, (NCHUNK // 2) * NT, stored, 0)
-
 
 def per_device(query_gate, key_gate, value_input, decay_rates, residues, skip_gain, out_weight):
     dma = pltpu.SemaphoreType.DMA
     out = pl.pallas_call(
         kernel,
-        out_shape=jax.ShapeDtypeStruct((NB, NJ, COLS), BF16),
+        out_shape=pltpu.VMEM((NB, NJ, COLS), BF16),
         in_specs=[pl.BlockSpec(memory_space=pl.ANY)] * 7,
-        out_specs=pl.BlockSpec(memory_space=pl.ANY),
+        out_specs=pl.BlockSpec(memory_space=pltpu.VMEM),
         scratch_shapes=[
             pltpu.VMEM((ROWS, CHAN), BF16),
             pltpu.VMEM((ROWS, CHAN), BF16),
@@ -365,7 +385,6 @@
             pltpu.VMEM((COLS // LANES, ROWS, LANES), F32),
             pltpu.VMEM((COLS // LANES, ROWS, LANES), F32),
             pltpu.VMEM((COLS // LANES, ROWS, LANES), F32),
-            pltpu.VMEM((NB, NJ, COLS), BF16),
             pltpu.VMEM((NCG, MODES, NB, LANES), F32),
             pltpu.VMEM((NCG, MODES, NB, LANES), F32),
             pltpu.VMEM((NCG, MODES, NB, LANES), F32),
@@ -376,12 +395,12 @@
             pltpu.VMEM((8, CPS, MODES, LANES), F32),
             pltpu.VMEM((CPS, MODES, LANES), F32),
             pltpu.VMEM((8, CPS, MODES, LANES), F32),
-            dma((4, SHARES)), dma((2, NT)), dma((NCHUNK // 2, NT)),
+            dma((4, SHARES)), dma((2, NT)),
             dma((8,)), dma((8,)), dma((8,)), dma((8,)), dma((8,)), dma((8,)),
             dma((NCHUNK, NT)), dma((NCHUNK, NT)),
         ],
         compiler_params=pltpu.CompilerParams(
-            collective_id=0, has_side_effects=True, vmem_limit_bytes=60 * 2**20
+            collective_id=0, has_side_effects=True, vmem_limit_bytes=56 * 2**20
         ),
     )(
         query_gate, key_gate, value_input, decay_rates, residues, skip_gain.reshape(1, CHAN), out_weight

time: 126 us -> 121 us (0.960)
  Pallas kernels: 122 us -> 119 us
  local copies, waits for them, and re-layouts: 3.16 us -> 1.32 us
    pallas_call x1, Pallas kernels: 122 us -> 119 us  [per_device(): pl.pallas_call(kernel, out_shape=pltpu.VMEM((NB, NJ, COLS), BF16), in_spe...]
    unnamed x1, local copies, waits for them, and re-layouts: 3.16 us -> 1.32 us
where the time goes in v1:
time: 121 us
  Pallas kernels  119 us (98%)
  local copies, waits for them, and re-layouts  1.32 us (1%)
    pallas_call x1, Pallas kernels, per_device(): pl.pallas_call(kernel, out_shape=pltpu.VMEM((NB, NJ, COLS), BF16), in_spe...  119 us

profile of v1, /device:TPU:1, one launch (start us, length us, event | category | flops | bytes accessed | tf_op | source)
XLA Modules:
  0.0 120.6 jit_solution(405139701756596463)
XLA Ops:
  0.0 119.3 %shard_map.73 = bf16[8,64,2048]{2,1,0:T(8,128)(2,1)S(1)} custom-call(bf16[512,2048]{1,0:T(8,128)(2,1)} %q_hbm.1, bf16[512,2048]{1,0:T(8,128)(2,1)} %k_hbm.1, bf16[512,2048]{1,0:T(8,128)(2,1)} %v_hbm.1, f32[16,2048]{1,0:T(8,128)} %lam_hbm.1, f32[16,2048]{1,0:T(8,128)} %res_hbm.1, f32[1,2048]{1,0:T(1,128)} %bitcast.3, bf16[2048,4096]{1,0:T(8,128)(2,1)} %w_hbm.1), custom_call_target="tpu_custom_call" | custom-call | tf_op jit(solution)/shard_map/pallas_call | solution.py:369
  119.3 1.3 %copy.9 = bf16[512,2048]{1,0:T(8,128)(2,1)} copy(bf16[512,2048]{1,0:T(8,128)(2,1)S(1)} %bitcast.2) | data formatting | bytes 4194304

commit v2 on v1

--- a/solution.py
+++ b/solution.py
@@ -102,18 +102,19 @@
             cols = lanes(s * CPS + u)
             rate = lam[:, cols]
             a8 = spread(jnp.exp(-8.0 * rate))
+            a16 = a8 * a8
 
             def step(i, acc):
                 rows = pl.ds(pl.multiple_of(i * 16, 16), 16)
                 p = kb[rows, cols].astype(F32) * vb[rows, cols].astype(F32)
-                acc = acc * a8 + p[None, :8]
-                return acc * a8 + p[None, 8:]
-
-            acc = lax.fori_loop(0, ROWS // 16, step, jnp.zeros((MODES, NB, LANES), F32), unroll=8)
+                return acc * a16 + (p[None, :8] * a8 + p[None, 8:])
+
+            acc = lax.fori_loop(0, ROWS // 16, step, jnp.zeros((MODES, NB, LANES), F32), unroll=32)
             ends[s, u] = jnp.sum(acc * jnp.exp(spread(rate) * (sub - 7).astype(F32)), axis=1)
             return 0
 
-        lax.fori_loop(0, CPS, group_pass, 0)
+        for u in range(CPS):
+            group_pass(u, 0)
 
     def give_share(s):
         @pl.when(s != member)
@@ -278,7 +279,7 @@
             send_sem=sp.at[chunk, n], recv_sem=rp.at[chunk, n], device_id=partner, device_id_type=MESH,
         )
 
-    def project(chunk):
+    def project(chunk, first=0):
         rows = chunk_rows(chunk)
 
         def other(n, _):
@@ -288,7 +289,7 @@
             piece(chunk, n).start()
             return 0
 
-        lax.fori_loop(0, NT, other, 0)
+        lax.fori_loop(first, NT, other, 0)
 
     def project_own(chunk):
         rows = chunk_rows(chunk)
@@ -301,22 +302,33 @@
 
         lax.fori_loop(0, NT, own, 0)
 
-    for i in range(8):
-        s = lax.rem(member + i, 8)
-        if i > 0:
+    def begin(s, _):
+        @pl.when(s != member)
+        def _():
             wait_recv(recv3, r3, s, s3)
 
-        def start(u, _, s=s):
+        def start(u, _):
             cg = s * CPS + u
             state[cg] = state[cg] + pw_s[cg] * spread(recv3[s, u])
             second_pass(0, cg)
             return 0
 
-        lax.fori_loop(0, CPS, start, 0)
-
-    for n in range(NT):
+        return lax.fori_loop(0, CPS, start, 0)
+
+    ready = (SHARES - 2) * CPS * LANES
+    lax.fori_loop(0, SHARES - 2, begin, 0)
+    load_w(0, 0).wait()
+    early = jnp.dot(gated[:CROWS, :ready], wv[0, 0, :ready, :], preferred_element_type=F32)
+    for u in range(LPT):
+        send_p[u, :CROWS, :] = early[:, u * LANES:(u + 1) * LANES]
+    lax.fori_loop(SHARES - 2, SHARES, begin, 0)
+    late = jnp.dot(gated[:CROWS, ready:], wv[0, 0, ready:, :], preferred_element_type=F32)
+    for u in range(LPT):
+        send_p[u, :CROWS, :] += late[:, u * LANES:(u + 1) * LANES]
+    piece(0, 0).start()
+    for n in range(1, NT):
         load_w(0, n).wait()
-    project(0)
+    project(0, 1)
     for n in range(NT):
         load_w(1, n).wait()
     project_own(0)

time: 121 us -> 120 us (level)
  no operation moved by 1% of the time
where the time goes in v2:
time: 120 us
  Pallas kernels  118 us (98%)
  local copies, waits for them, and re-layouts  1.32 us (1%)
    pallas_call x1, Pallas kernels, per_device(): pl.pallas_call(kernel, out_shape=pltpu.VMEM((NB, NJ, COLS), BF16), in_spe...  118 us

profile of v2, /device:TPU:1, one launch (start us, length us, event | category | flops | bytes accessed | tf_op | source)
XLA Modules:
  0.0 119.7 jit_solution(15821439896641136628)
XLA Ops:
  0.0 118.4 %shard_map.73 = bf16[8,64,2048]{2,1,0:T(8,128)(2,1)S(1)} custom-call(bf16[512,2048]{1,0:T(8,128)(2,1)} %q_hbm.1, bf16[512,2048]{1,0:T(8,128)(2,1)} %k_hbm.1, bf16[512,2048]{1,0:T(8,128)(2,1)} %v_hbm.1, f32[16,2048]{1,0:T(8,128)} %lam_hbm.1, f32[16,2048]{1,0:T(8,128)} %res_hbm.1, f32[1,2048]{1,0:T(1,128)} %bitcast.3, bf16[2048,4096]{1,0:T(8,128)(2,1)} %w_hbm.1), custom_call_target="tpu_custom_call" | custom-call | tf_op jit(solution)/shard_map/pallas_call | solution.py:381
  118.4 1.3 %copy.9 = bf16[512,2048]{1,0:T(8,128)(2,1)} copy(bf16[512,2048]{1,0:T(8,128)(2,1)S(1)} %bitcast.2) | data formatting | bytes 4194304

commit v3 on v2

--- a/solution.py
+++ b/solution.py
@@ -26,7 +26,7 @@
 NT = COLS // TILE
 LPT = TILE // LANES
 EARLY = 4
-SPLIT1, SPLIT2 = 6, 15
+SPLIT1, SPLIT2 = 4, 13
 
 
 def one_minus_exp_neg(y):
@@ -345,20 +345,6 @@
 
     lax.fori_loop(1, NCHUNK, chunk_step, 0)
 
-    def finish(i, _):
-        h, n = i // NT, lax.rem(i, NT)
-        piece(2 * h, n).wait_recv()
-        piece(2 * h + 1, n).wait_recv()
-
-        for u in range(LPT):
-            k = n * LPT + u
-            for b in range(NB):
-                rows = pl.ds(h * (2 * CROWS) + b, 16, stride=NB)
-                out_v[b, pl.ds(pl.multiple_of(h * 16, 16), 16), lanes(k)] = (own_p[k, rows, :] + recv_p[k, rows, :]).astype(BF16)
-        return 0
-
-    lax.fori_loop(0, (NCHUNK // 2) * NT, finish, 0)
-
     for i in range(1, 8):
         m = lax.rem(member + i, 8)
         g = lax.rem(group + i, 8)
@@ -369,11 +355,19 @@
         copy2(g).wait_send()
         copy3(m).wait_send()
 
-    def drain(i, _):
-        piece(i // NT, lax.rem(i, NT)).wait_send()
-        return 0
-
-    lax.fori_loop(0, NCHUNK * NT, drain, 0)
+    def finish(i, _):
+        h, n = i // NT, lax.rem(i, NT)
+        piece(2 * h, n).wait()
+        piece(2 * h + 1, n).wait()
+
+        for u in range(LPT):
+            k = n * LPT + u
+            for b in range(NB):
+                rows = pl.ds(h * (2 * CROWS) + b, 16, stride=NB)
+                out_v[b, pl.ds(pl.multiple_of(h * 16, 16), 16), lanes(k)] = (own_p[k, rows, :] + recv_p[k, rows, :]).astype(BF16)
+        return 0
+
+    lax.fori_loop(0, (NCHUNK // 2) * NT, finish, 0)
 
 
 def per_device(query_gate, key_gate, value_input, decay_rates, residues, skip_gain, out_weight):

time: 120 us -> 118 us (0.983)
    pallas_call x1, Pallas kernels: 118 us -> 117 us  [per_device(): pl.pallas_call(kernel, out_shape=pltpu.VMEM((NB, NJ, COLS), BF16), in_spe...]
where the time goes in v3:
time: 118 us
  Pallas kernels  117 us (99%)
  local copies, waits for them, and re-layouts  1.32 us (1%)
    pallas_call x1, Pallas kernels, per_device(): pl.pallas_call(kernel, out_shape=pltpu.VMEM((NB, NJ, COLS), BF16), in_spe...  117 us

profile of v3, /device:TPU:1, one launch (start us, length us, event | category | flops | bytes accessed | tf_op | source)
XLA Modules:
  0.0 117.9 jit_solution(9031198405962691772)
XLA Ops:
  0.0 116.6 %shard_map.73 = bf16[8,64,2048]{2,1,0:T(8,128)(2,1)S(1)} custom-call(bf16[512,2048]{1,0:T(8,128)(2,1)} %q_hbm.1, bf16[512,2048]{1,0:T(8,128)(2,1)} %k_hbm.1, bf16[512,2048]{1,0:T(8,128)(2,1)} %v_hbm.1, f32[16,2048]{1,0:T(8,128)} %lam_hbm.1, f32[16,2048]{1,0:T(8,128)} %res_hbm.1, f32[1,2048]{1,0:T(1,128)} %bitcast.3, bf16[2048,4096]{1,0:T(8,128)(2,1)} %w_hbm.1), custom_call_target="tpu_custom_call" | custom-call | tf_op jit(solution)/shard_map/pallas_call | solution.py:375
  116.6 1.3 %copy.9 = bf16[512,2048]{1,0:T(8,128)(2,1)} copy(bf16[512,2048]{1,0:T(8,128)(2,1)S(1)} %bitcast.2) | data formatting | bytes 4194304
